TPU v7x, 32 devices: a whole 2x2x4 slice. The times are simulated.
32 devices in a mesh: dp: 4 (over z), section: 2 (over core), mp: 4 (over y, x).
Axes of the slice: x: 2, y: 2, z: 4, core: 2. Of those that a mesh axis runs over, the one named last changes fastest.
Arguments:
- frames: bfloat16 [4, 128, 512], P('dp'), may hold values from -6 to 6
- lengths: int32 [4], P('dp'), may hold values from 32 to 128
- feature_proj: bfloat16 [512, 1920], P(None, 'mp'), may hold values from -0.25 to 0.25
- norm_gain: float32 [2, 1920], P('section'), may hold values from 0.25 to 1.75
- qkv_weight: bfloat16 [2, 1920, 5760], P('section', 'dp', 'mp'), may hold values from -0.125 to 0.125
- out_weight: bfloat16 [2, 1920, 1920], P('section', 'mp', 'dp'), may hold values from -0.125 to 0.125
- center: float32 [1920], replicated, may hold values from -4 to 4
- whitening: float32 [1920, 1024], P(None, 'dp'), may hold values from -0.125 to 0.125
Outputs:
- embeddings: float32 [4, 1024], P(None, 'dp')
All inputs are finite; a program needn't handle non-finite values.
Results may differ from a plain program's by a relative error of at most 0.0095.
Values may be sent and summed in bfloat16 or wider, within the bound.
A program may use at most 64 MiB of HBM per device.

v0:
```python
import functools

import jax
import jax.numpy as jnp
from jax import lax
from jax.experimental import pallas as pl
from jax.experimental.pallas import tpu as pltpu
from jax.sharding import PartitionSpec as P

MESH = pl.DeviceIdType.MESH
BF16 = jnp.bfloat16
F32 = jnp.float32

HD = 120


def passed_along(x, axis, by):
    count = lax.axis_size(axis)
    pairs = [(i, i + by) for i in range(count) if 0 <= i + by < count]
    return lax.ppermute(x, axis, pairs)


def broadcast(value, axis, source):
    kept = jnp.where(lax.axis_index(axis) == source, value, 0).astype(value.dtype)
    return lax.psum(kept, axis)


def layer_norm(values, gain):
    mean = jnp.mean(values, axis=-1, keepdims=True)
    centered = values - mean
    var = jnp.mean(centered * centered, axis=-1, keepdims=True)
    return centered * lax.rsqrt(var + 1e-05) * gain


def body(frames, lengths, feature_proj, norm_gain, qkv_weight, out_weight, center, whitening):
    section_index = lax.axis_index("section")
    gain = norm_gain[0]
    qkv_local = qkv_weight[0]
    out_local = out_weight[0]
    count_utt = frames.shape[0]
    frames_count = frames.shape[1]
    width = gain.shape[0]
    qkv_cols = qkv_local.shape[1]
    heads_local = qkv_cols // (3 * HD)
    full_qkv, full_out = (
        lax.all_gather(qkv_local, "dp", axis=0, tiled=True),
        lax.all_gather(out_local, "dp", axis=1, tiled=True),
    )
    received = jnp.zeros((frames_count, width), jnp.bfloat16)
    pooled_rows = []
    frame_ids = jnp.arange(frames_count, dtype=jnp.int32)
    for step in range(count_utt + 1):
        first_mb = min(step, count_utt - 1)
        second_mb = max(step - 1, 0)
        projected_part = jnp.dot(
            frames[first_mb], feature_proj, preferred_element_type=jnp.float32
        ).astype(jnp.bfloat16)
        projected = lax.all_gather(projected_part, "mp", axis=1, tiled=True)
        first_section = section_index == 0
        layer_input = jnp.where(first_section, projected, received)
        length = jnp.where(first_section, lengths[first_mb], lengths[second_mb])
        normed = layer_norm(layer_input.astype(jnp.float32), gain).astype(jnp.bfloat16)
        qkv_sum = jnp.dot(normed, full_qkv, preferred_element_type=jnp.float32)
        qkv = qkv_sum.astype(jnp.bfloat16).reshape(frames_count, 3, heads_local, HD)
        query = qkv[:, 0]
        keys = qkv[:, 1]
        values = qkv[:, 2]
        scores = jnp.einsum(
            "qhd,khd->hqk", query, keys, preferred_element_type=jnp.float32
        ) / jnp.sqrt(jnp.float32(HD))
        attention_valid = jnp.arange(frames_count, dtype=jnp.int32) < length
        scores = jnp.where(attention_valid[None, None, :], scores, jnp.float32(-1e30))
        probs = jax.nn.softmax(scores, axis=-1).astype(jnp.bfloat16)
        context = jnp.einsum(
            "hqk,khd->qhd", probs, values, preferred_element_type=jnp.float32
        ).astype(jnp.bfloat16)
        context = context.reshape(frames_count, heads_local * HD)
        partial_out = jnp.dot(context, full_out, preferred_element_type=jnp.float32)
        attended = lax.psum(partial_out.astype(jnp.bfloat16), "mp").astype(jnp.float32)
        result = (layer_input.astype(jnp.float32) + attended).astype(jnp.bfloat16)
        if step >= 1:
            valid = frame_ids < lengths[step - 1]
            summed = jnp.sum(
                jnp.where(valid[:, None], result.astype(jnp.float32), jnp.float32(0.0)), axis=0
            )
            pooled_rows.append(summed / lengths[step - 1].astype(jnp.float32))
        if step < count_utt:
            received = passed_along(result, "section", 1)
    pooled = jnp.stack(pooled_rows, axis=0)
    pooled = broadcast(pooled, "section", 1)
    return jnp.dot(
        lax.all_gather(pooled, "dp", axis=0, tiled=True) - center,
        whitening,
        precision=lax.Precision.HIGHEST,
        preferred_element_type=jnp.float32,
    )


def slice_of(row, index, count, size):
    value = jnp.zeros((1, size), F32)
    for part in range(count):
        value += jnp.where(index == part, row[:, part * size : (part + 1) * size], 0.0)
    return value


def three_parts(value):
    high = value.astype(BF16).astype(F32)
    rest = value - high
    middle = rest.astype(BF16).astype(F32)
    return high, middle, rest - middle


def whole_lanes(columns):
    return -(-columns // 128) * 128


def kernel(
    n,
    lengths_ref,
    frames_hbm,
    proj_hbm,
    gain_hbm,
    center_hbm,
    qkv_hbm,
    out_hbm,
    white_hbm,
    emb_ref,
    frames_ref,
    proj_ref,
    gain_ref,
    center_ref,
    wq,
    wq2,
    wo,
    wo2,
    wh,
    wh3,
    gsend,
    gsum,
    x0buf,
    xbuf,
    stat,
    normed,
    qkv,
    own,
    qsend,
    qrecv,
    sumsend,
    sumrecv,
    ctx,
    psend,
    precv,
    xnew,
    pool,
    rows,
    load_sem,
    x_send,
    x_recv,
    stat_send,
    stat_recv,
    g_send,
    g_recv,
    q_send,
    q_recv,
    sum_send,
    sum_recv,
    c_send,
    c_recv,
    p_send,
    p_recv,
    n_send,
    pool_send,
    pool_recv,
    row_send,
    row_recv,
):
    d = lax.axis_index("dp")
    s = lax.axis_index("section")
    m = lax.axis_index("mp")
    pieces, part_rows, lanes_x = xbuf.shape
    wide = wo.shape[1]
    frames_count = 2 * part_rows
    full = n * wide
    half = n // 2 * HD
    lanes_h = ctx.shape[3]
    pad_x, pad_h = lanes_x - wide, lanes_h - half
    groups = 2
    my_utt, my_half = d // 2, lax.rem(d, 2)
    pairs = (
        (frames_hbm, frames_ref),
        (proj_hbm, proj_ref.at[pl.ds(0, wide)]),
        (gain_hbm, gain_ref),
        (qkv_hbm, wq),
        (out_hbm, wo),
        (center_hbm, center_ref),
        (white_hbm, wh),
    )
    loads = [pltpu.make_async_copy(src, dst, load_sem.at[i]) for i, (src, dst) in enumerate(pairs)]
    for load in loads:
        load.start()

    barrier = pltpu.get_barrier_semaphore()
    for dz in range(n):
        for dm in range(n):
            if dz or dm:
                pl.semaphore_signal(
                    barrier, inc=1, device_id=(lax.rem(d + dz, n), s, lax.rem(m + dm, n)), device_id_type=MESH
                )
    for dm in range(n):
        pl.semaphore_signal(barrier, inc=1, device_id=(d, 1 - s, lax.rem(m + dm, n)), device_id_type=MESH)

    proj_ref[wide:] = jnp.zeros((pad_x, proj_ref.shape[1]), BF16)
    wq2[...] = jnp.zeros(wq2.shape, BF16)
    wo2[...] = jnp.zeros(wo2.shape, BF16)
    loads[0].wait()
    loads[1].wait()

    @pl.when(s == 0)
    def _():
        projected = lax.dot_general(
            frames_ref[0], proj_ref[...], (((1,), (1,)), ((), ())), preferred_element_type=F32
        ).astype(BF16)
        x0buf[0] = projected[:part_rows]
        x0buf[1] = projected[part_rows:]

    pl.semaphore_wait(barrier, n * n - 1 + n)

    def remote(src, dst, send, recv, target):
        return pltpu.make_async_remote_copy(
            src_ref=src, dst_ref=dst, send_sem=send, recv_sem=recv, device_id=target, device_id_type=MESH
        )

    def arrived(dst, recv):
        remote(dst, dst, x_send.at[0], recv, (d, s, m)).wait_recv()

    def above(k):
        return lax.rem(d + k, n), s, m

    def below(k):
        return lax.rem(d - k + n, n)

    sent = []

    def x0_copy(dm):
        return remote(
            x0buf, xbuf.at[pl.ds(2 * d, 2)], x_send.at[dm], x_recv.at[2 * d], (m, s, lax.rem(m + dm, n))
        )

    @pl.when(s == 0)
    def _():
        for dm in range(1, n):
            x0_copy(dm).start()

        @pl.when(d != m)
        def _():
            x0_copy(0).start()

        @pl.when(d == m)
        def _():
            xbuf[pl.ds(2 * d, 2)] = x0buf[...]

    loads[2].wait()
    gain = jnp.concatenate([slice_of(gain_ref, d, n, wide), jnp.zeros((1, pad_x), F32)], axis=1)
    ids = lax.broadcasted_iota(jnp.int32, (16, lanes_x), 0)
    gain_rows = jnp.zeros((16, lanes_x), F32)
    for part, value in enumerate(three_parts(gain)):
        gain_rows = jnp.where(ids == part, value, gain_rows)
    gain_rows = gain_rows.astype(BF16)
    loads[3].wait()
    for h in range(2):
        for t in range(3):
            start = (2 * t + h) * half
            wq2[h, 0:wide, t * lanes_h : t * lanes_h + half] = wq[:, start : start + half]
        products = jnp.dot(gain_rows, wq2[h], preferred_element_type=F32)
        gsend[h] = products[0:1] + products[1:2] + products[2:3]
    gsum[d] = gsend[my_half]
    for k in range(1, n):
        copy = remote(gsend.at[lax.rem(d + k, 2)], gsum.at[d], g_send.at[k], g_recv.at[d], above(k))
        copy.start()
        sent.append(copy)

    loads[4].wait()
    for h in range(2):
        wo2[h, 0:half, 0:wide] = wo[h * half : (h + 1) * half]

    def split_whitening():
        loads[6].wait()
        for part in range(n):
            for i, value in enumerate(three_parts(wh[part * wide : (part + 1) * wide])):
                wh3[i, part, 0:wide] = value.astype(BF16)
                wh3[i, part, wide:] = jnp.zeros((pad_x, wh3.shape[3]), BF16)

    @pl.when(s == 1)
    def _():
        split_whitening()

    lanes = lax.broadcasted_iota(jnp.int32, (frames_count, 128), 1)
    length_row = 4
    real = lax.broadcasted_iota(jnp.int32, (frames_count, lanes_x), 1) < wide

    def q_copy(g):
        return remote(qsend.at[g], qrecv.at[g], q_send.at[g], q_recv.at[g], (d + 1 - 2 * my_half, s, m))

    def sum_copy(g):
        return remote(sumsend.at[g], sumrecv.at[g], sum_send.at[g], sum_recv.at[g], above(2))

    def stat_copy(g, k):
        return remote(stat.at[g, d], stat.at[g, d], stat_send.at[g, k], stat_recv.at[g, d], above(k))

    def project(g):
        for i in range(2):
            u = 2 * g + i

            @pl.when(jnp.logical_and(s == 0, jnp.logical_or(d != u, m != d)))
            def _():
                arrived(xbuf.at[pl.ds(2 * u, 2)], x_recv.at[2 * u])

            @pl.when(s == 1)
            def _():
                arrived(xbuf.at[2 * u], x_recv.at[2 * u])
                arrived(xbuf.at[2 * u + 1], x_recv.at[2 * u + 1])

        table = jnp.zeros((frames_count, 128), F32)
        for i in range(2):
            u = 2 * g + i
            x = jnp.concatenate([xbuf[2 * u], xbuf[2 * u + 1]], axis=0).astype(F32)
            mean = jnp.sum(x, axis=1, keepdims=True) * (1.0 / wide)
            centered = jnp.where(real, x - mean, 0.0)
            spread = jnp.sum(centered * centered, axis=1, keepdims=True)
            table = jnp.where(lanes == 2 * i, mean, table)
            table = jnp.where(lanes == 2 * i + 1, spread, table)
            normed[g, i * frames_count : (i + 1) * frames_count] = (centered * gain).astype(BF16)
        table = jnp.where(lanes == length_row, lengths_ref[0].astype(F32), table)
        partial = jnp.dot(normed[g], wq2[1 - my_half], preferred_element_type=F32).astype(BF16)
        for i in range(2):
            qsend[g, i] = partial[i * frames_count : (i + 1) * frames_count]
        q_copy(g).start()
        stat[g, d] = table.T[0:8]
        for k in range(1, n):
            stat_copy(g, k).start()
        kept = jnp.dot(normed[g], wq2[my_half], preferred_element_type=F32)
        for i in range(2):
            own[g, i] = kept[i * frames_count : (i + 1) * frames_count]

    def exchange(g):
        arrived(qrecv.at[g], q_recv.at[g])
        other = 1 - my_utt
        sumsend[g] = (own[g, other] + qrecv[g, other].astype(F32)).astype(BF16)
        sum_copy(g).start()
        own[g, my_utt] = own[g, my_utt] + qrecv[g, my_utt].astype(F32)

    stat_ids = lax.broadcasted_iota(jnp.int32, (8, 128), 0)
    columns = lax.broadcasted_iota(jnp.int32, (frames_count, lanes_h), 1)
    keys_ids = lax.broadcasted_iota(jnp.int32, (frames_count, frames_count), 1).astype(F32)

    def attend(g):
        for k in range(1, n):
            arrived(stat.at[g, below(k)], stat_recv.at[g, below(k)])
            if g == 0:
                arrived(gsum.at[below(k)], g_recv.at[below(k)])

        def stat_row(k, row):
            return jnp.sum(jnp.where(stat_ids == row, stat[g, k], 0.0), axis=0, keepdims=True)

        slice_means = [stat_row(k, 2 * my_utt) for k in range(n)]
        mean = sum(slice_means) * (1.0 / n)
        deltas = [value - mean for value in slice_means]
        spread = sum(stat_row(k, 2 * my_utt + 1) for k in range(n)) + wide * sum(value * value for value in deltas)
        rstd = lax.rsqrt(spread * (1.0 / full) + 1e-05)
        by_row = jnp.zeros((8, 128), F32)
        for k, value in enumerate(deltas + [rstd]):
            by_row = jnp.where(stat_ids == k, value, by_row)
        by_frame = jnp.concatenate([by_row, jnp.zeros((frames_count - 8, 128), F32)], axis=0).T
        length = stat[g, 2 * g + my_utt, length_row : length_row + 1, :]
        valid = keys_ids < length
        arrived(sumrecv.at[g], sum_recv.at[g])
        summed = own[g, my_utt] + sumrecv[g].astype(F32)
        for k in range(n):
            summed = summed + by_frame[:, k : k + 1] * gsum[k]
        qkv[g] = (summed * by_frame[:, n : n + 1]).astype(BF16)
        query = qkv[g, :, 0:lanes_h]
        keys = qkv[g, :, lanes_h : 2 * lanes_h]
        values = qkv[g, :, 2 * lanes_h : 3 * lanes_h]
        context = jnp.zeros((frames_count, lanes_h), F32)
        for h in range(half // HD):
            in_head = jnp.logical_and(columns >= h * HD, columns < (h + 1) * HD)
            head_query = jnp.where(in_head, query, jnp.zeros_like(query))
            head_values = jnp.where(in_head, values, jnp.zeros_like(values))
            scores = lax.dot_general(
                head_query, keys, (((1,), (1,)), ((), ())), preferred_element_type=F32
            ) / jnp.sqrt(F32(HD))
            scores = jnp.where(valid, scores, F32(-1e30))
            weights = jnp.exp(scores - jnp.max(scores, axis=1, keepdims=True))
            probs = (weights / jnp.sum(weights, axis=1, keepdims=True)).astype(BF16)
            context += jnp.dot(probs, head_values, preferred_element_type=F32)
        ctx[g, d] = context.astype(BF16)
        for k in (2, 1, 3):
            copy = remote(ctx.at[g, d], ctx.at[g, d], c_send.at[g, k], c_recv.at[g, d], above(k))
            copy.start()
            sent.append(copy)

    def p_copy(g, to):
        return remote(psend.at[g, to], precv.at[g, m], p_send.at[g, to], p_recv.at[g, m], (d, s, to))

    def put_out(g):
        for i in range(2):
            total = jnp.zeros((frames_count, lanes_x), F32)
            for h in range(2):
                source = 2 * i + h

                @pl.when(d != source)
                def _():
                    arrived(ctx.at[g, source], c_recv.at[g, source])

                total += jnp.dot(ctx[g, source], wo2[h], preferred_element_type=F32)
            total = total.astype(BF16)
            for h in range(2):
                to = 2 * i + h
                psend[g, to] = total[h * part_rows : (h + 1) * part_rows]

                @pl.when(m != to)
                def _():
                    p_copy(g, to).start()

                @pl.when(m == to)
                def _():
                    precv[g, to] = psend[g, to]

    def next_copy(g, dm):
        return remote(
            xnew.at[g], xbuf.at[n * g + m], n_send.at[g, dm], x_recv.at[n * g + m], (d, 1, lax.rem(m + dm, n))
        )

    def pool_copy(g, ds, dm):
        return remote(
            pool.at[g, m],
            pool.at[g, m],
            pool_send.at[g, ds, dm],
            pool_recv.at[g, m],
            (d, lax.rem(s + ds, 2), lax.rem(m + dm, n)),
        )

    hops = [(ds, dm) for ds in range(2) for dm in range(n) if ds or dm]

    def finish(g):
        for k in range(1, n):
            source = lax.rem(m - k + n, n)
            arrived(precv.at[g, source], p_recv.at[g, source])
        attended = precv[g, 0].astype(F32)
        for k in range(1, n):
            attended = attended + precv[g, k].astype(F32)
        xnew[g] = (xbuf[n * g + m].astype(F32) + attended).astype(BF16)

        @pl.when(s == 0)
        def _():
            for dm in range(n):
                next_copy(g, dm).start()

        @pl.when(s == 1)
        def _():
            length = stat[g, 2 * g + m // 2, length_row : length_row + 1, :]
            frame = lax.broadcasted_iota(jnp.int32, (8, part_rows), 1) + part_rows * lax.rem(m, 2)
            weights = jnp.where(frame.astype(F32) < length[:, :part_rows], 1.0, 0.0).astype(BF16)
            pool[g, m] = jnp.dot(weights, xnew[g], preferred_element_type=F32)
            for ds, dm in hops:
                pool_copy(g, ds, dm).start()

    project(0)

    @pl.when(s == 0)
    def _():
        project(1)

    exchange(0)
    attend(0)

    @pl.when(s == 0)
    def _():
        exchange(1)

    @pl.when(s == 1)
    def _():
        project(1)

    put_out(0)

    @pl.when(s == 1)
    def _():
        exchange(1)

    finish(0)
    attend(1)
    put_out(1)
    finish(1)

    @pl.when(s == 0)
    def _():
        split_whitening()

    loads[5].wait()
    row_ids = lax.broadcasted_iota(jnp.int32, (8, lanes_x), 0)
    gathered = jnp.zeros((8, lanes_x), F32)
    for u in range(n):
        g, i = u // 2, u % 2
        for source in (2 * i, 2 * i + 1):
            @pl.when(jnp.logical_or(s == 0, m != source))
            def _():
                arrived(pool.at[g, source], pool_recv.at[g, source])

        total = pool[g, 2 * i] + pool[g, 2 * i + 1]
        length = stat[g, u, length_row : length_row + 1, 0:1]
        gathered = jnp.where(row_ids == u, total / length, gathered)
    center = slice_of(center_ref[...].reshape(1, full), d, n, wide)
    rows[d] = gathered - jnp.concatenate([center, jnp.zeros((1, pad_x), F32)], axis=1)
    for k in range(1, n):
        copy = remote(rows.at[d], rows.at[d], row_send.at[k], row_recv.at[d], above(k))
        copy.start()
        sent.append(copy)
    for k in range(1, n):
        arrived(rows.at[below(k)], row_recv.at[below(k)])
    result = jnp.zeros((32, emb_ref.shape[1]), F32)
    for part in range(n):
        parts = jnp.concatenate(list(three_parts(rows[part])) + [jnp.zeros((8, lanes_x), F32)], axis=0).astype(BF16)
        for i in range(3):
            result += jnp.dot(
                parts, wh3[i, part], preferred_element_type=F32
            )
    result = result[0:8] + result[8:16] + result[16:24]
    emb_ref[...] = result[0:n]

    for copy in sent:
        copy.wait_send()
    for g in range(groups):
        for k in range(1, n):
            stat_copy(g, k).wait_send()
        q_copy(g).wait_send()
        sum_copy(g).wait_send()
        for to in range(n):
            @pl.when(m != to)
            def _():
                p_copy(g, to).wait_send()

    @pl.when(s == 0)
    def _():
        for dm in range(1, n):
            x0_copy(dm).wait_send()

        @pl.when(d != m)
        def _():
            x0_copy(0).wait_send()

        for g in range(groups):
            for dm in range(n):
                next_copy(g, dm).wait_send()

    @pl.when(s == 1)
    def _():
        for g in range(groups):
            for ds, dm in hops:
                pool_copy(g, ds, dm).wait_send()


def fused(n, frames, lengths, feature_proj, norm_gain, qkv_weight, out_weight, center, whitening):
    frames_count = frames.shape[1]
    wide = feature_proj.shape[1]
    qkv_cols = qkv_weight.shape[2]
    head_rows = out_weight.shape[1]
    out_cols = whitening.shape[1]
    rows, lanes_x, lanes_h = frames_count // 2, whole_lanes(wide), whole_lanes(head_rows // 2)
    columns = 3 * lanes_h
    vmem = pl.BlockSpec(memory_space=pltpu.VMEM)
    anywhere = pl.BlockSpec(memory_space=pl.ANY)
    dma = pltpu.SemaphoreType.DMA
    return pl.pallas_call(
        functools.partial(kernel, n),
        out_shape=jax.ShapeDtypeStruct((n, out_cols), F32),
        in_specs=[pl.BlockSpec(memory_space=pltpu.SMEM)] + [anywhere] * 7,
        out_specs=vmem,
        scratch_shapes=[
            pltpu.VMEM(frames.shape, BF16),
            pltpu.VMEM((lanes_x, feature_proj.shape[0]), BF16),
            pltpu.VMEM(norm_gain.shape, F32),
            pltpu.VMEM(center.shape, F32),
            pltpu.VMEM((wide, qkv_cols), BF16),
            pltpu.VMEM((2, lanes_x, columns), BF16),
            pltpu.VMEM((head_rows, wide), BF16),
            pltpu.VMEM((2, lanes_h, lanes_x), BF16),
            pltpu.VMEM((n * wide, out_cols), F32),
            pltpu.VMEM((3, n, lanes_x, out_cols), BF16),
            pltpu.VMEM((2, 1, columns), F32),
            pltpu.VMEM((n, 1, columns), F32),
            pltpu.VMEM((2, rows, lanes_x), BF16),
            pltpu.VMEM((2 * n, rows, lanes_x), BF16),
            pltpu.VMEM((2, n, 8, 128), F32),
            pltpu.VMEM((2, 2 * frames_count, lanes_x), BF16),
            pltpu.VMEM((2, frames_count, columns), BF16),
            pltpu.VMEM((2, 2, frames_count, columns), F32),
            pltpu.VMEM((2, 2, frames_count, columns), BF16),
            pltpu.VMEM((2, 2, frames_count, columns), BF16),
            pltpu.VMEM((2, frames_count, columns), BF16),
            pltpu.VMEM((2, frames_count, columns), BF16),
            pltpu.VMEM((2, n, frames_count, lanes_h), BF16),
            pltpu.VMEM((2, n, rows, lanes_x), BF16),
            pltpu.VMEM((2, n, rows, lanes_x), BF16),
            pltpu.VMEM((2, rows, lanes_x), BF16),
            pltpu.VMEM((2, n, 8, lanes_x), F32),
            pltpu.VMEM((n, 8, lanes_x), F32),
            dma((7,)),
            dma((n,)), dma((2 * n,)),
            dma((2, n)), dma((2, n)),
            dma((n,)), dma((n,)),
            dma((2,)), dma((2,)),
            dma((2,)), dma((2,)),
            dma((2, n)), dma((2, n)),
            dma((2, n)), dma((2, n)),
            dma((2, n)),
            dma((2, 2, n)), dma((2, n)),
            dma((n,)), dma((n,)),
        ],
        compiler_params=pltpu.CompilerParams(
            collective_id=0, has_side_effects=True, vmem_limit_bytes=60 * 1024 * 1024
        ),
    )(
        lengths,
        frames,
        feature_proj.T,
        norm_gain,
        center,
        qkv_weight.reshape(qkv_weight.shape[1:]),
        out_weight.reshape(out_weight.shape[1:]),
        whitening,
    )


def solution(mesh):
    in_specs = (
        P("dp", None, None),
        P("dp"),
        P(None, "mp"),
        P("section", None),
        P("section", "dp", "mp"),
        P("section", "mp", "dp"),
        P(),
        P(None, "dp"),
    )
    out_specs = P(None, "dp")

    def step(frames, lengths, feature_proj, norm_gain, qkv_weight, out_weight, center, whitening):
        n = mesh.shape["mp"]
        square = mesh.shape["dp"] == n and mesh.shape["section"] == 2
        square = square and n == 4 and frames.shape[0] == 1 and frames.shape[1] == 128
        square = square and qkv_weight.shape[2] == 3 * n * HD and qkv_weight.shape[1] == feature_proj.shape[1]
        if square:
            return fused(
                n, frames, lengths, feature_proj, norm_gain, qkv_weight, out_weight, center, whitening
            )
        return body(frames, lengths, feature_proj, norm_gain, qkv_weight, out_weight, center, whitening)

    return jax.shard_map(step, mesh=mesh, in_specs=in_specs, out_specs=out_specs, check_vma=False)
```

profile of v0, /device:TPU:0, one launch (start us, length us, event | category | flops | bytes accessed | tf_op | source)
XLA Modules:
  0.0 101.1 jit_solution(16992547069812586521)
XLA Ops:
  0.7 99.2 %shard_map.82 = f32[4,256]{1,0:T(4,128)} custom-call(s32[1]{0:T(128)S(6)} %copy.10.lengths_ref, bf16[1,128,512]{2,1,0:T(8,128)(2,1)} %frames_hbm.1, bf16[480,512]{1,0:T(8,128)(2,1)} %bitcast.4, f32[1,1920]{1,0:T(1,128)} %gain_hbm.1, f32[1920]{0:T(1024)} %center_hbm.1, bf16[480,1440]{1,0:T(8,128)(2,1)} %bitcast.3, bf16[480,480]{1,0:T(8,128)(2,1)} %bitcast.5, ...), custom_call_target="tpu_custom_call" | custom-call | tf_op jit(solution)/shard_map/pallas_call | solution.py:574
  99.9 1.3 %copy.11 = f32[4,256]{1,0:T(4,128)} copy(f32[4,256]{1,0:T(4,128)} %shard_map.82) | data formatting | bytes 8192
where the time goes:
time: 101 us
  Pallas kernels  99.2 us (98%)
  local copies, waits for them, and re-layouts  1.28 us (1%)
    pallas_call x1, Pallas kernels, fused(): pl.pallas_call(functools.partial(kernel, n), out_shape=jax.ShapeDtypeStru...  99.2 us

commit v1 on v0

--- a/solution.py
+++ b/solution.py
@@ -267,10 +267,17 @@
         gain_rows = jnp.where(ids == part, value, gain_rows)
     gain_rows = gain_rows.astype(BF16)
     loads[3].wait()
-    for h in range(2):
-        for t in range(3):
-            start = (2 * t + h) * half
-            wq2[h, 0:wide, t * lanes_h : t * lanes_h + half] = wq[:, start : start + half]
+
+    @pl.loop(0, wide // 32)
+    def _(step):
+        run = pl.ds(pl.multiple_of(step * 32, 32), 32)
+        for h in range(2):
+            for t in range(3):
+                start = (2 * t + h) * half
+                wq2[h, run, t * lanes_h : t * lanes_h + half] = wq[run, start : start + half]
+
+    @pl.loop(0, 2)
+    def _(h):
         products = jnp.dot(gain_rows, wq2[h], preferred_element_type=F32)
         gsend[h] = products[0:1] + products[1:2] + products[2:3]
     gsum[d] = gsend[my_half]
@@ -286,9 +293,15 @@
     def split_whitening():
         loads[6].wait()
         for part in range(n):
-            for i, value in enumerate(three_parts(wh[part * wide : (part + 1) * wide])):
-                wh3[i, part, 0:wide] = value.astype(BF16)
+            for i in range(3):
                 wh3[i, part, wide:] = jnp.zeros((pad_x, wh3.shape[3]), BF16)
+
+            @pl.loop(0, wide // 32)
+            def _(step):
+                source = pl.ds(pl.multiple_of(part * wide + step * 32, 32), 32)
+                target = pl.ds(pl.multiple_of(step * 32, 32), 32)
+                for i, value in enumerate(three_parts(wh[source])):
+                    wh3[i, part, target] = value.astype(BF16)
 
     @pl.when(s == 1)
     def _():
@@ -353,11 +366,12 @@
     columns = lax.broadcasted_iota(jnp.int32, (frames_count, lanes_h), 1)
     keys_ids = lax.broadcasted_iota(jnp.int32, (frames_count, frames_count), 1).astype(F32)
 
+    def ctx_copy(g, k):
+        return remote(ctx.at[g, d], ctx.at[g, d], c_send.at[g, k], c_recv.at[g, d], above(k))
+
     def attend(g):
         for k in range(1, n):
             arrived(stat.at[g, below(k)], stat_recv.at[g, below(k)])
-            if g == 0:
-                arrived(gsum.at[below(k)], g_recv.at[below(k)])
 
         def stat_row(k, row):
             return jnp.sum(jnp.where(stat_ids == row, stat[g, k], 0.0), axis=0, keepdims=True)
@@ -395,9 +409,7 @@
             context += jnp.dot(probs, head_values, preferred_element_type=F32)
         ctx[g, d] = context.astype(BF16)
         for k in (2, 1, 3):
-            copy = remote(ctx.at[g, d], ctx.at[g, d], c_send.at[g, k], c_recv.at[g, d], above(k))
-            copy.start()
-            sent.append(copy)
+            ctx_copy(g, k).start()
 
     def p_copy(g, to):
         return remote(psend.at[g, to], precv.at[g, m], p_send.at[g, to], p_recv.at[g, m], (d, s, to))
@@ -465,33 +477,26 @@
             for ds, dm in hops:
                 pool_copy(g, ds, dm).start()
 
-    project(0)
-
-    @pl.when(s == 0)
-    def _():
-        project(1)
-
-    exchange(0)
-    attend(0)
-
-    @pl.when(s == 0)
-    def _():
-        exchange(1)
-
-    @pl.when(s == 1)
-    def _():
-        project(1)
-
-    put_out(0)
-
-    @pl.when(s == 1)
-    def _():
-        exchange(1)
-
-    finish(0)
-    attend(1)
-    put_out(1)
-    finish(1)
+    @pl.loop(0, groups + 1)
+    def _(step):
+        @pl.when(step > 0)
+        def _():
+            exchange(step - 1)
+            attend(step - 1)
+
+        @pl.when(step < groups)
+        def _():
+            project(step)
+
+        @pl.when(step == 0)
+        def _():
+            for k in range(1, n):
+                arrived(gsum.at[below(k)], g_recv.at[below(k)])
+
+        @pl.when(step > 0)
+        def _():
+            put_out(step - 1)
+            finish(step - 1)
 
     @pl.when(s == 0)
     def _():
@@ -533,6 +538,7 @@
     for g in range(groups):
         for k in range(1, n):
             stat_copy(g, k).wait_send()
+            ctx_copy(g, k).wait_send()
         q_copy(g).wait_send()
         sum_copy(g).wait_send()
         for to in range(n):

time: 101 us -> 105 us (1.040)
  Pallas kernels: 99.2 us -> 103 us
    pallas_call x1, Pallas kernels: 99.2 us -> 103 us  [fused(): pl.pallas_call(functools.partial(kernel, n), out_shape=jax.ShapeDtypeStru...]
where the time goes in v1:
time: 105 us
  Pallas kernels  103 us (98%)
  local copies, waits for them, and re-layouts  1.28 us (1%)
    pallas_call x1, Pallas kernels, fused(): pl.pallas_call(functools.partial(kernel, n), out_shape=jax.ShapeDtypeStru...  103 us

profile of v1, /device:TPU:0, one launch (start us, length us, event | category | flops | bytes accessed | tf_op | source)
XLA Modules:
  0.0 105.2 jit_solution(18097543984324060816)
XLA Ops:
  0.7 103.3 %shard_map.82 = f32[4,256]{1,0:T(4,128)} custom-call(s32[1]{0:T(128)S(6)} %copy.10.lengths_ref, bf16[1,128,512]{2,1,0:T(8,128)(2,1)} %frames_hbm.1, bf16[480,512]{1,0:T(8,128)(2,1)} %bitcast.4, f32[1,1920]{1,0:T(1,128)} %gain_hbm.1, f32[1920]{0:T(1024)} %center_hbm.1, bf16[480,1440]{1,0:T(8,128)(2,1)} %bitcast.3, bf16[480,480]{1,0:T(8,128)(2,1)} %bitcast.5, ...), custom_call_target="tpu_custom_call" | custom-call | tf_op jit(solution)/shard_map/pallas_call | solution.py:580
  103.9 1.3 %copy.11 = f32[4,256]{1,0:T(4,128)} copy(f32[4,256]{1,0:T(4,128)} %shard_map.82) | data formatting | bytes 8192

commit v2 on v1

--- a/solution.py
+++ b/solution.py
@@ -479,9 +479,8 @@
 
     @pl.loop(0, groups + 1)
     def _(step):
-        @pl.when(step > 0)
-        def _():
-            exchange(step - 1)
+        @pl.when(jnp.logical_and(step > 0, s == 1))
+        def _():
             attend(step - 1)
 
         @pl.when(step < groups)
@@ -492,6 +491,14 @@
         def _():
             for k in range(1, n):
                 arrived(gsum.at[below(k)], g_recv.at[below(k)])
+
+        @pl.when(jnp.logical_and(step > 0, s == 0))
+        def _():
+            attend(step - 1)
+
+        @pl.when(step < groups)
+        def _():
+            exchange(step)
 
         @pl.when(step > 0)
         def _():

time: 105 us -> 101 us (0.962)
  Pallas kernels: 103 us -> 98.5 us
    pallas_call x1, Pallas kernels: 103 us -> 98.5 us  [fused(): pl.pallas_call(functools.partial(kernel, n), out_shape=jax.ShapeDtypeStru...]
where the time goes in v2:
time: 101 us; the launch traced here: 100 us
  Pallas kernels  98.5 us (98%)
  local copies, waits for them, and re-layouts  1.28 us (1%)
    pallas_call x1, Pallas kernels, fused(): pl.pallas_call(functools.partial(kernel, n), out_shape=jax.ShapeDtypeStru...  98.5 us

profile of v2, /device:TPU:0, one launch (start us, length us, event | category | flops | bytes accessed | tf_op | source)
XLA Modules:
  0.0 100.5 jit_solution(14747822000153541128)
XLA Ops:
  0.7 98.5 %shard_map.82 = f32[4,256]{1,0:T(4,128)} custom-call(s32[1]{0:T(128)S(6)} %copy.10.lengths_ref, bf16[1,128,512]{2,1,0:T(8,128)(2,1)} %frames_hbm.1, bf16[480,512]{1,0:T(8,128)(2,1)} %bitcast.4, f32[1,1920]{1,0:T(1,128)} %gain_hbm.1, f32[1920]{0:T(1024)} %center_hbm.1, bf16[480,1440]{1,0:T(8,128)(2,1)} %bitcast.3, bf16[480,480]{1,0:T(8,128)(2,1)} %bitcast.5, ...), custom_call_target="tpu_custom_call" | custom-call | tf_op jit(solution)/shard_map/pallas_call | solution.py:587
  99.2 1.3 %copy.11 = f32[4,256]{1,0:T(4,128)} copy(f32[4,256]{1,0:T(4,128)} %shard_map.82) | data formatting | bytes 8192

commit v3 on v2

--- a/solution.py
+++ b/solution.py
@@ -210,8 +210,6 @@
         pl.semaphore_signal(barrier, inc=1, device_id=(d, 1 - s, lax.rem(m + dm, n)), device_id_type=MESH)
 
     proj_ref[wide:] = jnp.zeros((pad_x, proj_ref.shape[1]), BF16)
-    wq2[...] = jnp.zeros(wq2.shape, BF16)
-    wo2[...] = jnp.zeros(wo2.shape, BF16)
     loads[0].wait()
     loads[1].wait()
 
@@ -259,6 +257,8 @@
         def _():
             xbuf[pl.ds(2 * d, 2)] = x0buf[...]
 
+    wq2[...] = jnp.zeros(wq2.shape, BF16)
+    wo2[...] = jnp.zeros(wo2.shape, BF16)
     loads[2].wait()
     gain = jnp.concatenate([slice_of(gain_ref, d, n, wide), jnp.zeros((1, pad_x), F32)], axis=1)
     ids = lax.broadcasted_iota(jnp.int32, (16, lanes_x), 0)

time: 101 us -> 101 us (level)
  no operation moved by 1% of the time
where the time goes in v3:
time: 101 us; the launch traced here: 100 us
  Pallas kernels  98.5 us (98%)
  local copies, waits for them, and re-layouts  1.28 us (1%)
    pallas_call x1, Pallas kernels, fused(): pl.pallas_call(functools.partial(kernel, n), out_shape=jax.ShapeDtypeStru...  98.5 us

profile of v3, /device:TPU:0, one launch (start us, length us, event | category | flops | bytes accessed | tf_op | source)
XLA Modules:
  0.0 100.5 jit_solution(6750085589626648662)
XLA Ops:
  0.7 98.5 %shard_map.82 = f32[4,256]{1,0:T(4,128)} custom-call(s32[1]{0:T(128)S(6)} %copy.10.lengths_ref, bf16[1,128,512]{2,1,0:T(8,128)(2,1)} %frames_hbm.1, bf16[480,512]{1,0:T(8,128)(2,1)} %bitcast.4, f32[1,1920]{1,0:T(1,128)} %gain_hbm.1, f32[1920]{0:T(1024)} %center_hbm.1, bf16[480,1440]{1,0:T(8,128)(2,1)} %bitcast.3, bf16[480,480]{1,0:T(8,128)(2,1)} %bitcast.5, ...), custom_call_target="tpu_custom_call" | custom-call | tf_op jit(solution)/shard_map/pallas_call | solution.py:587
  99.2 1.3 %copy.11 = f32[4,256]{1,0:T(4,128)} copy(f32[4,256]{1,0:T(4,128)} %shard_map.82) | data formatting | bytes 8192
